TPU v7x, 128 devices: a whole 4x4x4 slice. The times are simulated.
128 devices in a mesh: row: 32 (over z, x, core), col: 4 (over y).
Axes of the slice: x: 4, y: 4, z: 4, core: 2. Of those that a mesh axis runs over, the one named last changes fastest.
Arguments:
- blocks: bfloat16 [65536, 128, 128], P(('row', 'col')), may hold values from -0.046875 to 0.046875
- block_row: int32 [65536], P(('row', 'col')), may hold values from -1 to 7, as said below
- block_col: int32 [65536], P(('row', 'col')), may hold values from -1 to 31, as said below
- sketch: bfloat16 [524288, 128], P(('row', 'col')), may hold values from -6 to 6
Outputs:
- basis: float32 [32768, 128], P(('row', 'col'))
- factor: float32 [128, 128], replicated
Inputs may be any that keep to these rules, and one draw needn't show every extreme that they name: The 512 slots of one device form 32 groups of 16 consecutive slots; in each group the live slots come first, 1 to 16 of them, then padding marked -1 in block_row and block_col alike; in every draw some group of some device is full. `block_col`: no two live slots of one group of one device name the same pair of block row and block column offset.
All inputs are finite; a program needn't handle non-finite values.
Results may differ from a plain program's by a relative error of at most 0.0003.
Values may be sent and summed in bfloat16 or wider, within the bound.
A program may use at most 192 MiB of HBM per device.

v0:
```python
import jax
import jax.numpy as jnp
from jax import lax
from jax.sharding import PartitionSpec as P

BLK = 128
RANK = 128
BR_DEV = 8


def upper_factor(gram):
    order = gram.shape[0]
    columns = jnp.arange(order, dtype=jnp.int32)

    def one_row(index, upper):
        column = lax.dynamic_slice_in_dim(upper, index, 1, 1)[:, 0]
        gram_row = lax.dynamic_slice_in_dim(gram, index, 1, 0)[0]
        remain = gram_row - jnp.dot(column, upper, precision=lax.Precision.HIGHEST)
        pivot = lax.dynamic_slice_in_dim(remain, index, 1, 0)[0]
        new_row = jnp.where(columns >= index, remain / jnp.sqrt(pivot), jnp.zeros_like(remain))
        return lax.dynamic_update_slice_in_dim(upper, new_row[None, :], index, 0)

    return lax.fori_loop(0, order, one_row, jnp.zeros_like(gram))


def upper_inverse(upper):
    order = upper.shape[0]
    columns = jnp.arange(order, dtype=jnp.int32)

    def one_row(turn, inverse):
        index = order - 1 - turn
        upper_row = lax.dynamic_slice_in_dim(upper, index, 1, 0)[0]
        unit = (columns == index).astype(upper.dtype)
        remain = unit - jnp.dot(upper_row, inverse, precision=lax.Precision.HIGHEST)
        pivot = lax.dynamic_slice_in_dim(upper_row, index, 1, 0)[0]
        return lax.dynamic_update_slice_in_dim(inverse, (remain / pivot)[None, :], index, 0)

    return lax.fori_loop(0, order, one_row, jnp.zeros_like(upper))


def row_sums(blocks, chosen, block_row, block_rows):
    products = jnp.einsum("kab,kbc->kac", blocks, chosen, preferred_element_type=jnp.float32)
    selector = (block_row[None, :] == block_rows[:, None]).astype(jnp.float32)
    return jnp.einsum("bk,kac->bac", selector, products, precision=lax.Precision.HIGH)


def shards(blocks, block_row, block_col, sketch):
    row_count = lax.axis_size("row")
    slot_count = blocks.shape[0]
    capacity = slot_count // row_count
    shard_blocks = sketch.shape[0] // BLK
    block_rows = jnp.arange(BR_DEV, dtype=jnp.int32)
    gathered = lax.all_gather(sketch, "row", axis=0, tiled=True).reshape(
        row_count * shard_blocks, BLK, RANK
    )
    position = jnp.arange(slot_count, dtype=jnp.int32) // capacity * shard_blocks + jnp.clip(
        block_col, 0, shard_blocks - 1
    )
    partial_value = row_sums(blocks, gathered[position], block_row, block_rows)
    slab_rows = lax.psum_scatter(
        partial_value.reshape(BR_DEV * BLK, RANK), "col", scatter_dimension=0, tiled=True
    )
    gram_local = jnp.dot(slab_rows.T, slab_rows, precision=lax.Precision.HIGHEST)
    factor = upper_factor(lax.psum(gram_local, ("row", "col")))
    basis = jnp.dot(slab_rows, upper_inverse(factor), precision=lax.Precision.HIGHEST)
    return (basis, factor)


def solution(mesh):
    in_specs = (
        P(("row", "col"), None, None),
        P(("row", "col")),
        P(("row", "col")),
        P(("row", "col"), None),
    )
    out_specs = (P(("row", "col"), None), P())
    return jax.shard_map(shards, mesh=mesh, in_specs=in_specs, out_specs=out_specs, check_vma=False)
```

profile of v0, /device:TPU:1, one launch (start us, length us, event | category | flops | bytes accessed | tf_op | source)
XLA Modules:
  0.0 918.3 jit_solution(14056964549729659597)
XLA Ops:
  8.6 119.2 %all-gather.2.cloned.1.call-done = bf16[131072,128]{1,0:T(8,128)(2,1)} async-done(((bf16[4096,128]{1,0:T(8,128)(2,1)}), bf16[131072,128]{1,0:T(8,128)(2,1)}) %all-gather.2.cloned.1.call-update) | async-done | bytes 33554448 | tf_op jit(solution)/shard_map/all_gather | solution.py:53
  127.9 15.1 %gather_fusion = bf16[512,128,128]{2,1,0:T(8,128)(2,1)} fusion(bf16[1024,128,128]{2,1,0:T(8,128)(2,1)} %bitcast.61, s32[1024]{0:T(1024)S(1)} %pad_clamp_fusion), kind=kCustom, calls=%fused_computation | custom fusion | bytes 33556480 | tf_op jit(solution)/shard_map/gather | solution.py:59
  143.0 25.2 %fusion.24 = f32[512,128,128]{2,1,0:T(8,128)} fusion(bf16[512,128,128]{2,1,0:T(8,128)(2,1)} %gather_fusion, bf16[512,128,128]{2,1,0:T(8,128)(2,1)} %param.8), kind=kOutput, calls=%fused_computation.33 | convolution fusion | flops 2147483648 | bytes 67108864 | tf_op jit(solution)/shard_map/kab,kbc->kac/dot_general | solution.py:42
  168.1 33.4 %copy.15 = f32[512,128,128]{1,0,2:T(8,128)} copy(f32[512,128,128]{2,1,0:T(8,128)} %fusion.24) | data formatting | bytes 67108864 | tf_op jit(solution)/shard_map/kab,kbc->kac/dot_general | solution.py:42
  201.6 13.2 %fusion.14 = f32[8,128,128]{2,0,1:T(8,128)S(1)} fusion(f32[512,128,128]{1,0,2:T(8,128)} %copy.15, s32[512]{0:T(512)S(1)} %copy-done.1), kind=kOutput, calls=%fused_computation.17 | convolution fusion | flops 402657280 | bytes 34080768 | tf_op jit(solution)/shard_map/bk,kac->bac/dot_general | solution.py:44
  214.8 0.9 copy.11
  215.8 19.8 %reduce-scatter.2.cloned.1.call-done = f32[256,128]{1,0:T(8,128)} async-done(((f32[1024,128]{1,0:T(8,128)}), f32[256,128]{1,0:T(8,128)}) %reduce-scatter.2.cloned.1.call-update) | async-done | bytes 131088 | tf_op jit(solution)/shard_map/reduce_scatter | solution.py:60
  235.5 2.0 fusion.25
  237.6 142.5 %all-reduce.2.cloned.1.call-done = f32[128,128]{1,0:T(8,128)} async-done(((f32[128,128]{1,0:T(8,128)}), f32[128,128]{1,0:T(8,128)}) %all-reduce.2.cloned.1.call-update) | async-done | bytes 65552 | tf_op jit(solution)/shard_map/psum | solution.py:64
  380.1 344.5 %while.31 = (s32[]{:T(128)}, f32[128,128]{0,1:T(8,128)S(1)}, f32[128,128]{1,0:T(8,128)}, s32[]{:T(128)}, s32[]{:T(128)}) while((s32[]{:T(128)}, f32[128,128]{0,1:T(8,128)S(1)}, f32[128,128]{1,0:T(8,128)}, s32[]{:T(128)}, s32[]{:T(128)}) %tuple.78), condition=%wide.region_3.4_spmd.clone, body=%wide.region_2.3_spmd.clone.sunk | while | flops 197122 | bytes 71261 | solution.py:23
  466.1 0.9 fusion.44
  468.8 0.9 fusion.44
  471.5 0.9 fusion.44
  474.2 0.9 fusion.44
  476.9 0.9 fusion.44
  479.6 0.9 fusion.44
  482.3 0.9 fusion.44
  485.0 0.9 fusion.44
  681.4 0.9 fusion.44
  684.1 0.9 fusion.44
  686.8 0.9 fusion.44
  689.5 0.9 fusion.44
  724.7 185.3 %while.32 = (s32[]{:T(128)}, f32[128,128]{1,0:T(8,128)S(1)}, f32[128,128]{1,0:T(8,128)S(1)}, s32[]{:T(128)}, s32[]{:T(128)}, /*index=5*/s32[]{:T(128)}, s32[]{:T(128)}) while((s32[]{:T(128)}, f32[128,128]{1,0:T(8,128)S(1)}, f32[128,128]{1,0:T(8,128)S(1)}, s32[]{:T(128)}, s32[]{:T(128)}, /*index=5*/s32[]{:T(128)}, s32[]{:T(128)}) %tuple.81), condition=%wide.region_5.6_spmd.clone, body=%wide.region_4.5_spmd.clone.sunk | while | flops 197127 | bytes 67751 | solution.py:38
  910.0 1.8 fusion.26
  (1027 shorter events, 424.4 us)
Async XLA Ops:
  7.2 120.7 %all-gather.2.cloned.1.call-start = ((), (), s32[]{:S(2)}) async-start(), calls=%async_computation.1 | async-start | bytes 34603008 | tf_op jit(solution)/shard_map/all_gather | solution.py:53
  7.9 227.6 %reduce-scatter.2.cloned.1.call-start = ((), (), s32[]{:S(2)}) async-start(), calls=%async_computation.2 | async-start | bytes 655360 | tf_op jit(solution)/shard_map/reduce_scatter | solution.py:60
  168.1 33.5 %copy-start.1 = (s32[512]{0:T(512)S(1)}, s32[512]{0:T(512)}, u32[]{:S(2)}) copy-start(s32[512]{0:T(512)} %param.9) | copy-start | bytes 6148
  215.7 164.4 %all-reduce.2.cloned.1.call-start = ((), (), s32[]{:S(2)}) async-start(), calls=%async_computation.3 | async-start | bytes 131072 | tf_op jit(solution)/shard_map/psum | solution.py:64
  909.9 1.9 copy-start
Sparse Core Ops, SparseCore 0:
  10.3 117.5 all-gather.1
  215.8 19.6 reduce-scatter.1
  240.9 139.1 all-reduce.1
where the time goes:
time: 926 us; the launch traced here: 918 us
  waiting for transfers between devices  282 us (30%)
  local copies, waits for them, and re-layouts  271 us (29%)
  matrix products  253 us (27%)
  loops' own time  96.7 us (10%)
  between operations  13.8 us (1%)
    psum x1, waiting for transfers between devices, shards(): factor = upper_factor(lax.psum(gram_local, ('row', 'col')))  143 us
    all_gather x1, waiting for transfers between devices, shards(): lax.all_gather(sketch, 'row', axis=0, tiled=True)  119 us
    dot_general x128, matrix products, one_row(): remain = gram_row - jnp.dot(column, upper, precision=lax.Precision.HIGHEST)  109 us
    dot_general x128, matrix products, one_row(): remain = unit - jnp.dot(upper_row, inverse, precision=lax.Precision.HIGHEST)  102 us
    another operation x1, loops' own time, upper_factor(): return lax.fori_loop(0, order, one_row, jnp.zeros_like(gram))  92.7 us
    dynamic_slice x128, local copies, waits for them, and re-layouts, one_row(): pivot = lax.dynamic_slice_in_dim(remain, index, 1, 0)[0]  81.4 us
    dynamic_slice x128, local copies, waits for them, and re-layouts, one_row(): pivot = lax.dynamic_slice_in_dim(upper_row, index, 1, 0)[0]  75.3 us
    dynamic_update_slice x128, local copies, waits for them, and re-layouts, one_row(): return lax.dynamic_update_slice_in_dim(upper, new_row[None, :], index, 0)  45.9 us
  transfers between devices with their start and end apart: 3, of which 3 were waited for; matrix products, arithmetic and copies ran while one was open for 0% of the time, Pallas kernels for 0%

commit v1 on v0

v1 whole, which is shorter than its diff:
```python
import functools

import jax
import jax.numpy as jnp
from jax import lax
from jax.experimental import pallas as pl
from jax.experimental.pallas import tpu as pltpu
from jax.sharding import PartitionSpec as P

MESH = pl.DeviceIdType.MESH
BLK = 128
RANK = 128
BR_DEV = 8
CAP = 16
SIDE = 4
HIGHEST = lax.Precision.HIGHEST


def place():
    row = lax.axis_index("row")
    return row // 8, lax.rem(row // 2, SIDE), lax.rem(row, 2), lax.axis_index("col")


def row_of(z, x, core):
    return z * 8 + x * 2 + core


def gather_kernel(mine_ref, all_ref, local_sem, send_sem, recv_sem, pair_send, pair_recv):
    z, x, core, y = place()
    rows = mine_ref.shape[0]
    half, quarter = rows // 2, rows // 4

    barrier = pltpu.get_barrier_semaphore()

    def other(dz, dx):
        return (row_of(lax.rem(z + dz + SIDE, SIDE), lax.rem(x + dx + SIDE, SIDE), core), y)

    pair = (row_of(z, x, 1 - core), y)
    for peer in (other(0, 1), other(0, -1), other(1, 0), other(-1, 0), pair):
        pl.semaphore_signal(barrier, inc=1, device_id=peer, device_id_type=MESH)
    pl.semaphore_wait(barrier, 5)

    me = row_of(z, x, core)
    own = pltpu.make_async_copy(mine_ref, all_ref.at[me], local_sem)
    own.start()

    pending = []
    index = {}

    def slot(name):
        return index.setdefault(name, len(index))

    def shift(h, along, across):
        return (across, along) if h == 0 else (along, across)

    def piece(h, a, b, part):
        dz, dx = shift(h, -a, -b)
        source = row_of(lax.rem(z + dz + SIDE, SIDE), lax.rem(x + dx + SIDE, SIDE), core)
        start, size = {"all": (h * half, half), "lo": (h * half, quarter), "hi": (h * half + quarter, quarter)}[part]
        return source, pl.ds(start, size)

    def send(h, a, b, part, axis, step):
        source, span = piece(h, a, b, part)
        to = other(*(shift(h, step, 0) if axis == 0 else shift(h, 0, step)))
        there = (h, (a + step) % SIDE, b, part) if axis == 0 else (h, a, (b + step) % SIDE, part)
        s = slot(there)
        src = mine_ref.at[span] if (a, b) == (0, 0) else all_ref.at[source, span]
        copy = pltpu.make_async_remote_copy(
            src_ref=src, dst_ref=all_ref.at[source, span], send_sem=send_sem.at[s], recv_sem=recv_sem.at[s],
            device_id=to, device_id_type=MESH,
        )
        copy.start()
        pending.append(copy)

    def arrived(h, a, b, part):
        s = slot((h, a, b, part))
        source, span = piece(h, a, b, part)
        there = all_ref.at[source, span]
        pltpu.make_async_remote_copy(
            src_ref=there, dst_ref=there, send_sem=send_sem.at[s], recv_sem=recv_sem.at[s], device_id=pair,
            device_id_type=MESH,
        ).wait_recv()

    shared = []

    def share(h, a, b, part):
        s = len(shared)
        source, span = piece(h, a, b, part)
        src = mine_ref.at[span] if (a, b) == (0, 0) else all_ref.at[source, span]
        copy = pltpu.make_async_remote_copy(
            src_ref=src, dst_ref=all_ref.at[source, span], send_sem=pair_send.at[s], recv_sem=pair_recv.at[s],
            device_id=pair, device_id_type=MESH,
        )
        copy.start()
        flip, _ = piece(h, a, b, part)
        shared.append((copy, flip + 1 - 2 * core, span))

    for h in (0, 1):
        for step in (1, -1):
            send(h, 0, 0, "all", 0, step)
    for h in (0, 1):
        for step in (1, -1):
            send(h, 0, 0, "all", 1, step)
    for h in (0, 1):
        share(h, 0, 0, "all")
    for step in (1, -1):
        for h in (0, 1):
            a = step % SIDE
            arrived(h, a, 0, "all")
            send(h, a, 0, "lo" if step == 1 else "hi", 0, step)
            for onward in (1, -1):
                send(h, a, 0, "all", 1, onward)
            share(h, a, 0, "all")
    for h in (0, 1):
        arrived(h, 2, 0, "lo")
        arrived(h, 2, 0, "hi")
        for onward in (1, -1):
            send(h, 2, 0, "all", 1, onward)
        share(h, 2, 0, "all")
    for a in (0, 1, 3, 2):
        for step in (1, -1):
            for h in (0, 1):
                arrived(h, a, step % SIDE, "all")
                send(h, a, step % SIDE, "lo" if step == 1 else "hi", 1, step)
                share(h, a, step % SIDE, "all")
    for a in (0, 1, 3, 2):
        for h in (0, 1):
            for part in ("lo", "hi"):
                arrived(h, a, 2, part)
            share(h, a, 2, "all")
    own.wait()
    for copy in pending:
        copy.wait_send()
    for s, (copy, source, span) in enumerate(shared):
        copy.wait_send()
        there = all_ref.at[source, span]
        pltpu.make_async_remote_copy(
            src_ref=there, dst_ref=there, send_sem=pair_send.at[s], recv_sem=pair_recv.at[s], device_id=pair,
            device_id_type=MESH,
        ).wait_recv()


def gather(sketch):
    return pl.pallas_call(
        gather_kernel,
        out_shape=jax.ShapeDtypeStruct((32,) + sketch.shape, sketch.dtype),
        in_specs=[pl.BlockSpec(memory_space=pl.ANY)],
        out_specs=pl.BlockSpec(memory_space=pl.ANY),
        scratch_shapes=[
            pltpu.SemaphoreType.DMA,
            pltpu.SemaphoreType.DMA((48,)),
            pltpu.SemaphoreType.DMA((48,)),
            pltpu.SemaphoreType.DMA((32,)),
            pltpu.SemaphoreType.DMA((32,)),
        ],
        compiler_params=pltpu.CompilerParams(collective_id=0, has_side_effects=True),
    )(sketch)


def products_kernel(row_ref, col_ref, blocks_ref, sketch_ref, out_ref, total_ref):
    group = pl.program_id(0)

    @pl.when(group == 0)
    def _():
        total_ref[...] = jnp.zeros_like(total_ref)

    for k in range(CAP):
        row = row_ref[group * CAP + k]
        col = jnp.maximum(col_ref[group * CAP + k], 0)
        target = jnp.where(row < 0, BR_DEV, row)
        total_ref[target] += jnp.dot(blocks_ref[k], sketch_ref[0, col], preferred_element_type=jnp.float32)

    @pl.when(group == pl.num_programs(0) - 1)
    def _():
        out_ref[...] = total_ref[pl.ds(0, BR_DEV)]


def products(blocks, block_row, block_col, gathered):
    groups = gathered.shape[0]
    per = gathered.shape[1] // BLK
    return pl.pallas_call(
        products_kernel,
        out_shape=jax.ShapeDtypeStruct((BR_DEV, BLK, RANK), jnp.float32),
        grid_spec=pltpu.PrefetchScalarGridSpec(
            num_scalar_prefetch=2,
            grid=(groups,),
            in_specs=[
                pl.BlockSpec((CAP, BLK, BLK), lambda g, *_: (g, 0, 0)),
                pl.BlockSpec((1, per, BLK, RANK), lambda g, *_: (g, 0, 0, 0)),
            ],
            out_specs=pl.BlockSpec((BR_DEV, BLK, RANK), lambda g, *_: (0, 0, 0)),
            scratch_shapes=[pltpu.VMEM((BR_DEV + 1, BLK, RANK), jnp.float32)],
        ),
        compiler_params=pltpu.CompilerParams(vmem_limit_bytes=24 * 2**20),
    )(block_row, block_col, blocks, gathered.reshape(groups, per, BLK, RANK))


def reduce_kernel(part_ref, slab_ref, gram_ref, local_ref, col_buf, pair_buf, x_buf, z_buf, col_s, col_r, pair_s, pair_r, x_s, x_r, z_s, z_r, last_s, last_r):
    z, x, core, y = place()
    rows = slab_ref.shape[0]
    strip = RANK // 8
    me8 = y * 2 + core

    def octet(step):
        number = lax.rem(me8 + step, 8)
        return (row_of(z, x, lax.rem(number, 2)), number // 2), number

    def along_x(step):
        return (row_of(z, lax.rem(x + step, SIDE), core), y)

    def along_z(step):
        return (row_of(lax.rem(z + step, SIDE), x, core), y)

    barrier = pltpu.get_barrier_semaphore()
    for step in range(1, 8):
        pl.semaphore_signal(barrier, inc=1, device_id=octet(step)[0], device_id_type=MESH)
    for step in range(1, SIDE):
        pl.semaphore_signal(barrier, inc=1, device_id=along_x(step), device_id_type=MESH)
        pl.semaphore_signal(barrier, inc=1, device_id=along_z(step), device_id_type=MESH)
    pl.semaphore_wait(barrier, 13)

    sent = []

    def push(src, dst, send, recv, to):
        copy = pltpu.make_async_remote_copy(
            src_ref=src, dst_ref=dst, send_sem=send, recv_sem=recv, device_id=to, device_id_type=MESH
        )
        copy.start()
        sent.append(copy)
        return copy

    copies = []
    for step in (2, 1, 3):
        to = lax.rem(y + step, SIDE)
        copies.append(push(
            part_ref.at[pl.ds(to * rows, rows)], col_buf.at[step - 1], col_s.at[step - 1], col_r.at[step - 1],
            (lax.axis_index("row"), to),
        ))
    total = part_ref[pl.ds(y * rows, rows), :]
    for copy in copies:
        copy.wait_recv()
    total = total + (col_buf[0] + col_buf[1] + col_buf[2])
    slab_ref[...] = total
    local_ref[...] = lax.dot_general(
        total, total, (((0,), (0,)), ((), ())), precision=HIGHEST, preferred_element_type=jnp.float32
    )

    copies = []
    for step in range(1, 8):
        to, number = octet(step)
        copies.append(push(
            local_ref.at[pl.ds(number * strip, strip)], pair_buf.at[step - 1], pair_s.at[step - 1],
            pair_r.at[step - 1], to,
        ))
    part = local_ref[pl.ds(me8 * strip, strip), :]
    for step, copy in enumerate(copies):
        copy.wait_recv()
        part = part + pair_buf[step]

    for here, buf, send, recv, peer in ((x, x_buf, x_s, x_r, along_x), (z, z_buf, z_s, z_r, along_z)):
        buf[pl.ds(here, 1)] = part[None]
        copies = []
        for step in range(1, SIDE):
            copies.append(push(buf.at[here], buf.at[here], send.at[step - 1], recv.at[step - 1], peer(step)))
        for copy in copies:
            copy.wait_recv()
        part = (buf[0] + buf[1]) + (buf[2] + buf[3])

    mine = pl.ds(me8 * strip, strip)
    gram_ref[mine, :] = part
    for step in range(1, 8):
        to, number = octet(step)
        push(gram_ref.at[mine], gram_ref.at[mine], last_s.at[step - 1], last_r.at[step - 1], to)
    for copy in sent[-7:]:
        copy.wait_recv()
    for copy in sent:
        copy.wait_send()


def reduce(partial):
    rows = partial.shape[0] // SIDE
    dma = pltpu.SemaphoreType.DMA
    strip = RANK // 8
    f32 = jnp.float32
    return pl.pallas_call(
        reduce_kernel,
        out_shape=(jax.ShapeDtypeStruct((rows, RANK), f32), jax.ShapeDtypeStruct((RANK, RANK), f32)),
        in_specs=[pl.BlockSpec(memory_space=pltpu.VMEM)],
        out_specs=(pl.BlockSpec(memory_space=pltpu.VMEM),) * 2,
        scratch_shapes=[
            pltpu.VMEM((RANK, RANK), f32),
            pltpu.VMEM((3, rows, RANK), f32),
            pltpu.VMEM((7, strip, RANK), f32),
            pltpu.VMEM((SIDE, strip, RANK), f32),
            pltpu.VMEM((SIDE, strip, RANK), f32),
            dma((3,)), dma((3,)), dma((7,)), dma((7,)), dma((3,)), dma((3,)), dma((3,)), dma((3,)), dma((7,)), dma((7,)),
        ],
        compiler_params=pltpu.CompilerParams(collective_id=1, has_side_effects=True),
    )(partial)


def factor_kernel(gram_ref, slab_ref, basis_ref, factor_ref):
    tile = (8, RANK)
    count = RANK // 8
    lane = lax.broadcasted_iota(jnp.int32, tile, 1)
    sub = lax.broadcasted_iota(jnp.int32, tile, 0)
    left = [gram_ref[8 * i : 8 * i + 8, :] for i in range(count)]
    right = [jnp.where(lane == sub + 8 * i, 1.0, 0.0) for i in range(count)]
    inverse = []
    for p in range(count):
        cols = {
            (i, m): jnp.broadcast_to(left[i][:, 8 * p + m : 8 * p + m + 1], tile)
            for i in range(p, count)
            for m in range(8)
        }
        upper = jnp.zeros(tile, jnp.float32)
        lower = jnp.zeros(tile, jnp.float32)
        for k in range(8):
            pivot = jnp.broadcast_to(cols[p, k][k : k + 1, :], tile)
            scale = lax.rsqrt(pivot)
            row = jnp.broadcast_to(left[p][k : k + 1, :], tile) * scale
            inverse_row = jnp.broadcast_to(right[p][k : k + 1, :], tile) * scale
            upper = jnp.where(sub == k, row, upper)
            lower = jnp.where(sub == k, inverse_row, lower)
            ahead = {m: jnp.broadcast_to(cols[p, m][k : k + 1, :], tile) * scale for m in range(k + 1, 8)}
            for i in range(p, count):
                if i == p and k == 7:
                    continue
                weight = cols[i, k] * scale
                for m in range(k + 1, 8):
                    cols[i, m] = cols[i, m] - weight * ahead[m]
                left[i] = left[i] - weight * row
                right[i] = right[i] - weight * inverse_row
        factor_ref[8 * p : 8 * p + 8, :] = jnp.where(lane >= sub + 8 * p, upper, 0.0)
        inverse.append(lower)
    basis_ref[...] = lax.dot_general(
        slab_ref[...],
        jnp.concatenate(inverse, axis=0),
        (((1,), (1,)), ((), ())),
        precision=HIGHEST,
        preferred_element_type=jnp.float32,
    )


def factorise(gram, slab):
    return pl.pallas_call(
        factor_kernel,
        out_shape=(
            jax.ShapeDtypeStruct(slab.shape, jnp.float32),
            jax.ShapeDtypeStruct(gram.shape, jnp.float32),
        ),
    )(gram, slab)


def shards(blocks, block_row, block_col, sketch):
    gathered = gather(sketch)
    partial = products(blocks, block_row, block_col, gathered)
    slab, gram = reduce(partial.reshape(BR_DEV * BLK, RANK))
    return factorise(gram, slab)


def solution(mesh):
    in_specs = (
        P(("row", "col"), None, None),
        P(("row", "col")),
        P(("row", "col")),
        P(("row", "col"), None),
    )
    out_specs = (P(("row", "col"), None), P())
    return jax.shard_map(shards, mesh=mesh, in_specs=in_specs, out_specs=out_specs, check_vma=False)
```

time: 926 us -> 167 us (0.18)
  waiting for transfers between devices: 282 us -> 0 us
  local copies, waits for them, and re-layouts: 271 us -> 6.56 us
  matrix products: 253 us -> 0 us
  Pallas kernels: 0 us -> 159 us
  loops' own time: 96.7 us -> 0 us
  between operations: 13.8 us -> 0.7 us
    dot_general x260 -> x0, matrix products: 253 us -> none  [the longest x128 109 us: one_row(): remain = gram_row - jnp.dot(column, upper, precision=lax.Precision.HIGHEST)]
    pallas_call x0 -> x4, Pallas kernels: none -> 159 us  [the longest x1 97.3 us: gather(): pl.pallas_call(gather_kernel, out_shape=jax.ShapeDtypeStruct((32,) + sket...]
    dynamic_slice x256 -> x0, local copies, waits for them, and re-layouts: 157 us -> none  [the longest x128 81.4 us: one_row(): pivot = lax.dynamic_slice_in_dim(remain, index, 1, 0)[0]]
    psum x1 -> x0, waiting for transfers between devices: 143 us -> none  [shards(): factor = upper_factor(lax.psum(gram_local, ('row', 'col')))]
    all_gather x1 -> x0, waiting for transfers between devices: 119 us -> none  [shards(): lax.all_gather(sketch, 'row', axis=0, tiled=True)]
    another operation x2 -> x0, loops' own time: 96.7 us -> none  [the longest x1 92.7 us: upper_factor(): return lax.fori_loop(0, order, one_row, jnp.zeros_like(gram))]
    dynamic_update_slice x256 -> x0, local copies, waits for them, and re-layouts: 49.9 us -> none  [the longest x128 45.9 us: one_row(): return lax.dynamic_update_slice_in_dim(upper, new_row[None, :], index, 0)]
    dot_general x2 -> x0, local copies, waits for them, and re-layouts: 34.3 us -> none  [the longest x1 33.4 us: row_sums(): jnp.einsum('kab,kbc->kac', blocks, chosen, preferred_element_type=jnp.flo...]
  transfers between devices with their start and end apart: 3 -> 0, of which waited for: 3 -> 0; matrix products, arithmetic and copies ran while one was open for 0% -> 0% of each run, Pallas kernels for 0% -> 0%
where the time goes in v1:
time: 167 us; the launch traced here: 166 us
  Pallas kernels  159 us (95%)
  local copies, waits for them, and re-layouts  6.56 us (4%)
    pallas_call x1, Pallas kernels, gather(): pl.pallas_call(gather_kernel, out_shape=jax.ShapeDtypeStruct((32,) + sket...  97.3 us
    pallas_call x1, Pallas kernels, reduce(): pl.pallas_call(reduce_kernel, out_shape=(jax.ShapeDtypeStruct((rows, RANK...  28.5 us
    pallas_call x1, Pallas kernels, products(): pl.pallas_call(products_kernel, out_shape=jax.ShapeDtypeStruct((BR_DEV, B...  27.1 us
    unnamed x8, local copies, waits for them, and re-layouts  6.56 us
    pallas_call x1, Pallas kernels, factorise(): pl.pallas_call(factor_kernel, out_shape=(jax.ShapeDtypeStruct(slab.shape,...  5.78 us

profile of v1, /device:TPU:1, one launch (start us, length us, event | category | flops | bytes accessed | tf_op | source)
XLA Modules:
  0.0 165.9 jit_solution(6464812876707114374)
XLA Ops:
  0.6 0.0 copy-start.3
  0.6 0.0 copy-start.2
  0.7 97.3 %shard_map.59 = bf16[32,4096,128]{2,1,0:T(8,128)(2,1)} custom-call(bf16[4096,128]{1,0:T(8,128)(2,1)} %mine_ref.1), custom_call_target="tpu_custom_call" | custom-call | tf_op jit(solution)/shard_map/pallas_call | solution.py:144
  98.0 0.0 copy-done.3
  98.0 0.0 copy-done.2
  98.0 0.0 copy-start
  98.0 5.8 %copy-done = bf16[512,128,128]{2,1,0:T(8,128)(2,1)S(1)} copy-done((bf16[512,128,128]{2,1,0:T(8,128)(2,1)S(1)}, bf16[512,128,128]{2,1,0:T(8,128)(2,1)}, u32[]{:S(2)}) %copy-start) | copy-done | bytes 16777240
  103.8 27.1 %shard_map.60 = f32[8,128,128]{2,1,0:T(8,128)S(1)} custom-call(s32[512]{0:T(512)S(1)} %copy-done.2, s32[512]{0:T(512)S(1)} %copy-done.3, bf16[512,128,128]{2,1,0:T(8,128)(2,1)S(1)} %copy-done, bf16[32,32,128,128]{3,2,1,0:T(8,128)(2,1)} %bitcast.3), custom_call_target="tpu_custom_call" | custom-call | tf_op jit(solution)/shard_map/pallas_call | solution.py:181
  130.8 0.0 copy-start.1
  130.8 0.8 copy-done.1
  131.6 28.5 %shard_map.61 = (f32[256,128]{1,0:T(8,128)}, f32[128,128]{1,0:T(8,128)}) custom-call(f32[1024,128]{1,0:T(8,128)} %bitcast.2), custom_call_target="tpu_custom_call" | custom-call | tf_op jit(solution)/shard_map/pallas_call | solution.py:285
  160.1 5.8 %shard_map.62 = (f32[256,128]{1,0:T(8,128)}, f32[128,128]{1,0:T(8,128)}) custom-call(f32[128,128]{1,0:T(8,128)} %get-tuple-element.4.gram_ref, f32[256,128]{1,0:T(8,128)} %get-tuple-element.5.slab_ref), custom_call_target="tpu_custom_call" | custom-call | tf_op jit(solution)/shard_map/pallas_call | solution.py:346
Async XLA Ops:
  0.6 97.4 %copy-start.3 = (s32[512]{0:T(512)S(1)}, s32[512]{0:T(512)}, u32[]{:S(2)}) copy-start(s32[512]{0:T(512)} %col_ref.1) | copy-start | bytes 6148
  0.6 97.4 %copy-start.2 = (s32[512]{0:T(512)S(1)}, s32[512]{0:T(512)}, u32[]{:S(2)}) copy-start(s32[512]{0:T(512)} %row_ref.1) | copy-start | bytes 6148
  98.0 5.8 %copy-start = (bf16[512,128,128]{2,1,0:T(8,128)(2,1)S(1)}, bf16[512,128,128]{2,1,0:T(8,128)(2,1)}, u32[]{:S(2)}) copy-start(bf16[512,128,128]{2,1,0:T(8,128)(2,1)} %blocks_ref.1) | copy-start | bytes 50331652
  130.8 0.8 copy-start.1

commit v2 on v1

--- a/solution.py
+++ b/solution.py
@@ -25,10 +25,28 @@
     return z * 8 + x * 2 + core
 
 
-def gather_kernel(mine_ref, all_ref, local_sem, send_sem, recv_sem, pair_send, pair_recv):
+TURNS = (
+    (),
+    ((0, 1), (1, 0)),
+    ((0, 3),),
+    ((3, 0),),
+    ((1, 1),),
+    ((1, 3),),
+    ((3, 1),),
+    ((3, 3),),
+    (),
+    ((0, 2), (2, 0)),
+    ((1, 2), (2, 1)),
+    ((3, 2), (2, 3)),
+)
+
+
+def sampled_kernel(row_ref, col_ref, blocks_ref, mine_ref, total_ref, *scratch):
+    held = {(c // SIDE, c % SIDE): scratch[c] for c in range(SIDE * SIDE)}
+    stored, chain, block_sem, own_sem, send_sem, recv_sem, pair_send, pair_recv = scratch[SIDE * SIDE :]
     z, x, core, y = place()
-    rows = mine_ref.shape[0]
-    half, quarter = rows // 2, rows // 4
+    count = mine_ref.shape[0]
+    half, quarter = count // 2, count // 4
 
     barrier = pltpu.get_barrier_semaphore()
 
@@ -38,71 +56,92 @@
     pair = (row_of(z, x, 1 - core), y)
     for peer in (other(0, 1), other(0, -1), other(1, 0), other(-1, 0), pair):
         pl.semaphore_signal(barrier, inc=1, device_id=peer, device_id_type=MESH)
+    own = pltpu.make_async_copy(mine_ref, held[0, 0].at[0], own_sem)
+    own.start()
+    store = pltpu.make_async_copy(blocks_ref, stored, block_sem)
     pl.semaphore_wait(barrier, 5)
-
-    me = row_of(z, x, core)
-    own = pltpu.make_async_copy(mine_ref, all_ref.at[me], local_sem)
-    own.start()
 
     pending = []
     index = {}
 
-    def slot(name):
-        return index.setdefault(name, len(index))
-
-    def shift(h, along, across):
-        return (across, along) if h == 0 else (along, across)
-
-    def piece(h, a, b, part):
-        dz, dx = shift(h, -a, -b)
-        source = row_of(lax.rem(z + dz + SIDE, SIDE), lax.rem(x + dx + SIDE, SIDE), core)
+    def spot(h, a, b, part, plane):
         start, size = {"all": (h * half, half), "lo": (h * half, quarter), "hi": (h * half + quarter, quarter)}[part]
-        return source, pl.ds(start, size)
+        return held[(a, b) if h == 0 else (b, a)].at[plane, pl.ds(start, size)]
+
+    def origin(h, a, b, part):
+        if (a, b) == (0, 0):
+            return mine_ref.at[pl.ds(h * half, half)]
+        return spot(h, a, b, part, 0)
 
     def send(h, a, b, part, axis, step):
-        source, span = piece(h, a, b, part)
-        to = other(*(shift(h, step, 0) if axis == 0 else shift(h, 0, step)))
-        there = (h, (a + step) % SIDE, b, part) if axis == 0 else (h, a, (b + step) % SIDE, part)
-        s = slot(there)
-        src = mine_ref.at[span] if (a, b) == (0, 0) else all_ref.at[source, span]
+        shift = (step, 0) if axis == 0 else (0, step)
+        there = (h, (a + shift[0]) % SIDE, (b + shift[1]) % SIDE, part)
+        s = index.setdefault(there, len(index))
         copy = pltpu.make_async_remote_copy(
-            src_ref=src, dst_ref=all_ref.at[source, span], send_sem=send_sem.at[s], recv_sem=recv_sem.at[s],
-            device_id=to, device_id_type=MESH,
+            src_ref=origin(h, a, b, part), dst_ref=spot(*there, 0), send_sem=send_sem.at[s], recv_sem=recv_sem.at[s],
+            device_id=other(*(shift[::-1] if h == 0 else shift)), device_id_type=MESH,
         )
         copy.start()
         pending.append(copy)
 
     def arrived(h, a, b, part):
-        s = slot((h, a, b, part))
-        source, span = piece(h, a, b, part)
-        there = all_ref.at[source, span]
+        s = index[h, a, b, part]
+        there = spot(h, a, b, part, 0)
         pltpu.make_async_remote_copy(
             src_ref=there, dst_ref=there, send_sem=send_sem.at[s], recv_sem=recv_sem.at[s], device_id=pair,
             device_id_type=MESH,
         ).wait_recv()
 
-    shared = []
-
-    def share(h, a, b, part):
+    shared = {}
+
+    def share(h, a, b):
         s = len(shared)
-        source, span = piece(h, a, b, part)
-        src = mine_ref.at[span] if (a, b) == (0, 0) else all_ref.at[source, span]
         copy = pltpu.make_async_remote_copy(
-            src_ref=src, dst_ref=all_ref.at[source, span], send_sem=pair_send.at[s], recv_sem=pair_recv.at[s],
-            device_id=pair, device_id_type=MESH,
+            src_ref=origin(h, a, b, "all"), dst_ref=spot(h, a, b, "all", 1), send_sem=pair_send.at[s],
+            recv_sem=pair_recv.at[s], device_id=pair, device_id_type=MESH,
         )
         copy.start()
-        flip, _ = piece(h, a, b, part)
-        shared.append((copy, flip + 1 - 2 * core, span))
+        pending.append(copy)
+        shared[h, a, b] = copy
+
+    def multiply(dx, dz):
+        shared[0, dx, dz].wait_recv()
+        shared[1, dz, dx].wait_recv()
+        sketch = held[dx, dz]
+
+        def one_group(plane, _):
+            group = row_of(lax.rem(z - dz + SIDE, SIDE), lax.rem(x - dx + SIDE, SIDE), lax.rem(core + plane, 2))
+            last = [CAP] * BR_DEV
+            for k in range(CAP):
+                row = row_ref[group * CAP + k]
+                col = jnp.maximum(col_ref[group * CAP + k], 0)
+                before = CAP
+                for b in range(BR_DEV):
+                    same = row == b
+                    before = jnp.where(same, last[b], before)
+                    last[b] = jnp.where(same, k, last[b])
+                product = jnp.dot(stored[group, k], sketch[plane, col], preferred_element_type=jnp.float32)
+                chain[k] = product + chain[before]
+            for b in range(BR_DEV):
+                total_ref[b] += chain[last[b]]
+            return 0
+
+        lax.fori_loop(0, 2, one_group, 0)
 
     for h in (0, 1):
         for step in (1, -1):
             send(h, 0, 0, "all", 0, step)
     for h in (0, 1):
+        share(h, 0, 0)
+    for h in (0, 1):
         for step in (1, -1):
             send(h, 0, 0, "all", 1, step)
-    for h in (0, 1):
-        share(h, 0, 0, "all")
+    store.start()
+    total_ref[...] = jnp.zeros_like(total_ref)
+    chain[CAP] = jnp.zeros_like(chain[CAP])
+    own.wait()
+    store.wait()
+    multiply(0, 0)
     for step in (1, -1):
         for h in (0, 1):
             a = step % SIDE
@@ -110,89 +149,63 @@
             send(h, a, 0, "lo" if step == 1 else "hi", 0, step)
             for onward in (1, -1):
                 send(h, a, 0, "all", 1, onward)
-            share(h, a, 0, "all")
+            share(h, a, 0)
     for h in (0, 1):
         arrived(h, 2, 0, "lo")
         arrived(h, 2, 0, "hi")
         for onward in (1, -1):
             send(h, 2, 0, "all", 1, onward)
-        share(h, 2, 0, "all")
+        share(h, 2, 0)
+    turns = iter(TURNS)
     for a in (0, 1, 3, 2):
         for step in (1, -1):
             for h in (0, 1):
                 arrived(h, a, step % SIDE, "all")
                 send(h, a, step % SIDE, "lo" if step == 1 else "hi", 1, step)
-                share(h, a, step % SIDE, "all")
+                share(h, a, step % SIDE)
+            for chip in next(turns):
+                multiply(*chip)
     for a in (0, 1, 3, 2):
         for h in (0, 1):
             for part in ("lo", "hi"):
                 arrived(h, a, 2, part)
-            share(h, a, 2, "all")
-    own.wait()
+            share(h, a, 2)
+        for chip in next(turns):
+            multiply(*chip)
+    multiply(2, 2)
     for copy in pending:
         copy.wait_send()
-    for s, (copy, source, span) in enumerate(shared):
-        copy.wait_send()
-        there = all_ref.at[source, span]
-        pltpu.make_async_remote_copy(
-            src_ref=there, dst_ref=there, send_sem=pair_send.at[s], recv_sem=pair_recv.at[s], device_id=pair,
-            device_id_type=MESH,
-        ).wait_recv()
-
-
-def gather(sketch):
+
+
+def sample(blocks, block_row, block_col, sketch):
+    groups = blocks.shape[0] // CAP
+    count = sketch.shape[0] // BLK
+    dma = pltpu.SemaphoreType.DMA
     return pl.pallas_call(
-        gather_kernel,
-        out_shape=jax.ShapeDtypeStruct((32,) + sketch.shape, sketch.dtype),
-        in_specs=[pl.BlockSpec(memory_space=pl.ANY)],
-        out_specs=pl.BlockSpec(memory_space=pl.ANY),
-        scratch_shapes=[
-            pltpu.SemaphoreType.DMA,
-            pltpu.SemaphoreType.DMA((48,)),
-            pltpu.SemaphoreType.DMA((48,)),
-            pltpu.SemaphoreType.DMA((32,)),
-            pltpu.SemaphoreType.DMA((32,)),
+        sampled_kernel,
+        out_shape=jax.ShapeDtypeStruct((BR_DEV, BLK, RANK), jnp.float32),
+        in_specs=[
+            pl.BlockSpec(memory_space=pltpu.SMEM),
+            pl.BlockSpec(memory_space=pltpu.SMEM),
+            pl.BlockSpec(memory_space=pl.ANY),
+            pl.BlockSpec(memory_space=pl.ANY),
         ],
-        compiler_params=pltpu.CompilerParams(collective_id=0, has_side_effects=True),
-    )(sketch)
-
-
-def products_kernel(row_ref, col_ref, blocks_ref, sketch_ref, out_ref, total_ref):
-    group = pl.program_id(0)
-
-    @pl.when(group == 0)
-    def _():
-        total_ref[...] = jnp.zeros_like(total_ref)
-
-    for k in range(CAP):
-        row = row_ref[group * CAP + k]
-        col = jnp.maximum(col_ref[group * CAP + k], 0)
-        target = jnp.where(row < 0, BR_DEV, row)
-        total_ref[target] += jnp.dot(blocks_ref[k], sketch_ref[0, col], preferred_element_type=jnp.float32)
-
-    @pl.when(group == pl.num_programs(0) - 1)
-    def _():
-        out_ref[...] = total_ref[pl.ds(0, BR_DEV)]
-
-
-def products(blocks, block_row, block_col, gathered):
-    groups = gathered.shape[0]
-    per = gathered.shape[1] // BLK
-    return pl.pallas_call(
-        products_kernel,
-        out_shape=jax.ShapeDtypeStruct((BR_DEV, BLK, RANK), jnp.float32),
-        grid_spec=pltpu.PrefetchScalarGridSpec(
-            num_scalar_prefetch=2,
-            grid=(groups,),
-            in_specs=[
-                pl.BlockSpec((CAP, BLK, BLK), lambda g, *_: (g, 0, 0)),
-                pl.BlockSpec((1, per, BLK, RANK), lambda g, *_: (g, 0, 0, 0)),
-            ],
-            out_specs=pl.BlockSpec((BR_DEV, BLK, RANK), lambda g, *_: (0, 0, 0)),
-            scratch_shapes=[pltpu.VMEM((BR_DEV + 1, BLK, RANK), jnp.float32)],
+        out_specs=pl.BlockSpec(memory_space=pltpu.VMEM),
+        scratch_shapes=[pltpu.VMEM((2, count, BLK, RANK), sketch.dtype)] * (SIDE * SIDE)
+        + [
+            pltpu.VMEM((groups, CAP, BLK, BLK), blocks.dtype),
+            pltpu.VMEM((CAP + 1, BLK, RANK), jnp.float32),
+            dma,
+            dma,
+            dma((48,)),
+            dma((48,)),
+            dma((32,)),
+            dma((32,)),
+        ],
+        compiler_params=pltpu.CompilerParams(
+            collective_id=0, has_side_effects=True, vmem_limit_bytes=58 * 2**20
         ),
-        compiler_params=pltpu.CompilerParams(vmem_limit_bytes=24 * 2**20),
-    )(block_row, block_col, blocks, gathered.reshape(groups, per, BLK, RANK))
+    )(block_row, block_col, blocks.reshape(groups, CAP, BLK, BLK), sketch.reshape(count, BLK, RANK))
 
 
 def reduce_kernel(part_ref, slab_ref, gram_ref, local_ref, col_buf, pair_buf, x_buf, z_buf, col_s, col_r, pair_s, pair_r, x_s, x_r, z_s, z_r, last_s, last_r):
@@ -353,8 +366,7 @@
 
 
 def shards(blocks, block_row, block_col, sketch):
-    gathered = gather(sketch)
-    partial = products(blocks, block_row, block_col, gathered)
+    partial = sample(blocks, block_row, block_col, sketch)
     slab, gram = reduce(partial.reshape(BR_DEV * BLK, RANK))
     return factorise(gram, slab)
 

time: 167 us -> 134 us (0.80)
  Pallas kernels: 159 us -> 134 us
  local copies, waits for them, and re-layouts: 6.56 us -> 0 us
    pallas_call x2 -> x1, Pallas kernels: 124 us -> 99.6 us  [sample(): pl.pallas_call(sampled_kernel, out_shape=jax.ShapeDtypeStruct((BR_DEV, BL...]
    unnamed x8 -> x0, local copies, waits for them, and re-layouts: 6.56 us -> none
where the time goes in v2:
time: 134 us
  Pallas kernels  134 us (100%)
    pallas_call x1, Pallas kernels, sample(): pl.pallas_call(sampled_kernel, out_shape=jax.ShapeDtypeStruct((BR_DEV, BL...  99.6 us
    pallas_call x1, Pallas kernels, reduce(): pl.pallas_call(reduce_kernel, out_shape=(jax.ShapeDtypeStruct((rows, RANK...  28.2 us
    pallas_call x1, Pallas kernels, factorise(): pl.pallas_call(factor_kernel, out_shape=(jax.ShapeDtypeStruct(slab.shape,...  5.78 us

profile of v2, /device:TPU:1, one launch (start us, length us, event | category | flops | bytes accessed | tf_op | source)
XLA Modules:
  0.0 134.3 jit_solution(17973751930658769182)
XLA Ops:
  0.6 99.6 %shard_map.59 = f32[8,128,128]{2,1,0:T(8,128)} custom-call(s32[512]{0:T(512)} %row_ref.1, s32[512]{0:T(512)} %col_ref.1, bf16[32,16,128,128]{3,2,1,0:T(8,128)(2,1)} %bitcast.3, bf16[32,128,128]{2,1,0:T(8,128)(2,1)} %bitcast.5), custom_call_target="tpu_custom_call" | custom-call | tf_op jit(solution)/shard_map/pallas_call | solution.py:184
  100.2 28.2 %shard_map.60 = (f32[256,128]{1,0:T(8,128)}, f32[128,128]{1,0:T(8,128)}) custom-call(f32[1024,128]{1,0:T(8,128)} %bitcast.4), custom_call_target="tpu_custom_call" | custom-call | tf_op jit(solution)/shard_map/pallas_call | solution.py:298
  128.5 5.8 %shard_map.61 = (f32[256,128]{1,0:T(8,128)}, f32[128,128]{1,0:T(8,128)}) custom-call(f32[128,128]{1,0:T(8,128)} %get-tuple-element.4.gram_ref, f32[256,128]{1,0:T(8,128)} %get-tuple-element.5.slab_ref), custom_call_target="tpu_custom_call" | custom-call | tf_op jit(solution)/shard_map/pallas_call | solution.py:359

commit v3 on v2

--- a/solution.py
+++ b/solution.py
@@ -23,6 +23,10 @@
 
 def row_of(z, x, core):
     return z * 8 + x * 2 + core
+
+
+def far(step):
+    return sum(min(d, SIDE - d) for d in step)
 
 
 TURNS = (
@@ -41,9 +45,11 @@
 )
 
 
-def sampled_kernel(row_ref, col_ref, blocks_ref, mine_ref, total_ref, *scratch):
+def sampled_kernel(row_ref, col_ref, blocks_ref, mine_ref, slab_ref, gram_ref, *scratch):
     held = {(c // SIDE, c % SIDE): scratch[c] for c in range(SIDE * SIDE)}
-    stored, chain, block_sem, own_sem, send_sem, recv_sem, pair_send, pair_recv = scratch[SIDE * SIDE :]
+    stored, chain, total_ref, local_ref, col_buf, octet_buf, plane_buf, *scratch = scratch[SIDE * SIDE :]
+    block_sem, own_sem, send_sem, recv_sem, pair_send, pair_recv, *scratch = scratch
+    col_send, col_recv, octet_send, octet_recv, plane_send, plane_recv, last_send, last_recv = scratch
     z, x, core, y = place()
     count = mine_ref.shape[0]
     half, quarter = count // 2, count // 4
@@ -53,13 +59,19 @@
     def other(dz, dx):
         return (row_of(lax.rem(z + dz + SIDE, SIDE), lax.rem(x + dx + SIDE, SIDE), core), y)
 
+    me8 = y * 2 + core
+
+    def octet(step):
+        number = lax.rem(me8 + step, 8)
+        return (row_of(z, x, lax.rem(number, 2)), number // 2), number
+
     pair = (row_of(z, x, 1 - core), y)
-    for peer in (other(0, 1), other(0, -1), other(1, 0), other(-1, 0), pair):
+    for peer in (other(0, 1), other(0, -1), other(1, 0), other(-1, 0), *(octet(step)[0] for step in range(1, 8))):
         pl.semaphore_signal(barrier, inc=1, device_id=peer, device_id_type=MESH)
     own = pltpu.make_async_copy(mine_ref, held[0, 0].at[0], own_sem)
     own.start()
     store = pltpu.make_async_copy(blocks_ref, stored, block_sem)
-    pl.semaphore_wait(barrier, 5)
+    pl.semaphore_wait(barrier, 11)
 
     pending = []
     index = {}
@@ -173,6 +185,62 @@
         for chip in next(turns):
             multiply(*chip)
     multiply(2, 2)
+
+    def push(src, dst, send_to, recv_from, peer):
+        copy = pltpu.make_async_remote_copy(
+            src_ref=src, dst_ref=dst, send_sem=send_to, recv_sem=recv_from, device_id=peer, device_id_type=MESH
+        )
+        copy.start()
+        pending.append(copy)
+        return copy
+
+    share_rows = BR_DEV // SIDE
+    copies = []
+    for step in (2, 1, 3):
+        to = lax.rem(y + step, SIDE)
+        copies.append(push(
+            total_ref.at[pl.ds(to * share_rows, share_rows)], col_buf.at[step - 1], col_send.at[step - 1],
+            col_recv.at[step - 1], (lax.axis_index("row"), to),
+        ))
+    slab = total_ref[pl.ds(y * share_rows, share_rows)]
+    for copy in copies:
+        copy.wait_recv()
+    slab = (slab + (col_buf[0] + col_buf[1] + col_buf[2])).reshape(slab_ref.shape)
+    slab_ref[...] = slab
+    local_ref[...] = lax.dot_general(
+        slab, slab, (((0,), (0,)), ((), ())), precision=HIGHEST, preferred_element_type=jnp.float32
+    )
+
+    strip = RANK // 8
+    mine = pl.ds(me8 * strip, strip)
+    copies = []
+    for step in (4, 5, 3, 2, 6, 1, 7):
+        peer, number = octet(step)
+        copies.append(push(
+            local_ref.at[pl.ds(number * strip, strip)], octet_buf.at[step - 1], octet_send.at[step - 1],
+            octet_recv.at[step - 1], peer,
+        ))
+    for copy in copies:
+        copy.wait_recv()
+    part = local_ref[mine, :] + jnp.sum(octet_buf[...], axis=0)
+    me16 = z * SIDE + x
+    plane_buf[pl.ds(me16, 1)] = part[None]
+    copies = []
+    for dz, dx in sorted(((a, b) for a in range(SIDE) for b in range(SIDE) if a + b), key=far, reverse=True):
+        s = dz * SIDE + dx - 1
+        peer = other(dz, dx)
+        copies.append(push(plane_buf.at[me16], plane_buf.at[me16], plane_send.at[s], plane_recv.at[s], peer))
+    for copy in copies:
+        copy.wait_recv()
+    gram_ref[mine, :] = jnp.sum(plane_buf[...], axis=0)
+    copies = []
+    for step in (4, 5, 3, 2, 6, 1, 7):
+        peer, _ = octet(step)
+        copies.append(push(
+            gram_ref.at[mine], gram_ref.at[mine], last_send.at[step - 1], last_recv.at[step - 1], peer
+        ))
+    for copy in copies:
+        copy.wait_recv()
     for copy in pending:
         copy.wait_send()
 
@@ -180,136 +248,48 @@
 def sample(blocks, block_row, block_col, sketch):
     groups = blocks.shape[0] // CAP
     count = sketch.shape[0] // BLK
-    dma = pltpu.SemaphoreType.DMA
+    dma, f32 = pltpu.SemaphoreType.DMA, jnp.float32
     return pl.pallas_call(
         sampled_kernel,
-        out_shape=jax.ShapeDtypeStruct((BR_DEV, BLK, RANK), jnp.float32),
+        out_shape=(
+            jax.ShapeDtypeStruct((BR_DEV * BLK // SIDE, RANK), f32),
+            jax.ShapeDtypeStruct((RANK, RANK), f32),
+        ),
         in_specs=[
             pl.BlockSpec(memory_space=pltpu.SMEM),
             pl.BlockSpec(memory_space=pltpu.SMEM),
             pl.BlockSpec(memory_space=pl.ANY),
             pl.BlockSpec(memory_space=pl.ANY),
         ],
-        out_specs=pl.BlockSpec(memory_space=pltpu.VMEM),
+        out_specs=(pl.BlockSpec(memory_space=pltpu.VMEM),) * 2,
         scratch_shapes=[pltpu.VMEM((2, count, BLK, RANK), sketch.dtype)] * (SIDE * SIDE)
         + [
             pltpu.VMEM((groups, CAP, BLK, BLK), blocks.dtype),
-            pltpu.VMEM((CAP + 1, BLK, RANK), jnp.float32),
+            pltpu.VMEM((CAP + 1, BLK, RANK), f32),
+            pltpu.VMEM((BR_DEV, BLK, RANK), f32),
+            pltpu.VMEM((RANK, RANK), f32),
+            pltpu.VMEM((SIDE - 1, BR_DEV // SIDE, BLK, RANK), f32),
+            pltpu.VMEM((7, RANK // 8, RANK), f32),
+            pltpu.VMEM((SIDE * SIDE, RANK // 8, RANK), f32),
             dma,
             dma,
             dma((48,)),
             dma((48,)),
             dma((32,)),
             dma((32,)),
+            dma((3,)),
+            dma((3,)),
+            dma((7,)),
+            dma((7,)),
+            dma((15,)),
+            dma((15,)),
+            dma((7,)),
+            dma((7,)),
         ],
         compiler_params=pltpu.CompilerParams(
             collective_id=0, has_side_effects=True, vmem_limit_bytes=58 * 2**20
         ),
     )(block_row, block_col, blocks.reshape(groups, CAP, BLK, BLK), sketch.reshape(count, BLK, RANK))
-
-
-def reduce_kernel(part_ref, slab_ref, gram_ref, local_ref, col_buf, pair_buf, x_buf, z_buf, col_s, col_r, pair_s, pair_r, x_s, x_r, z_s, z_r, last_s, last_r):
-    z, x, core, y = place()
-    rows = slab_ref.shape[0]
-    strip = RANK // 8
-    me8 = y * 2 + core
-
-    def octet(step):
-        number = lax.rem(me8 + step, 8)
-        return (row_of(z, x, lax.rem(number, 2)), number // 2), number
-
-    def along_x(step):
-        return (row_of(z, lax.rem(x + step, SIDE), core), y)
-
-    def along_z(step):
-        return (row_of(lax.rem(z + step, SIDE), x, core), y)
-
-    barrier = pltpu.get_barrier_semaphore()
-    for step in range(1, 8):
-        pl.semaphore_signal(barrier, inc=1, device_id=octet(step)[0], device_id_type=MESH)
-    for step in range(1, SIDE):
-        pl.semaphore_signal(barrier, inc=1, device_id=along_x(step), device_id_type=MESH)
-        pl.semaphore_signal(barrier, inc=1, device_id=along_z(step), device_id_type=MESH)
-    pl.semaphore_wait(barrier, 13)
-
-    sent = []
-
-    def push(src, dst, send, recv, to):
-        copy = pltpu.make_async_remote_copy(
-            src_ref=src, dst_ref=dst, send_sem=send, recv_sem=recv, device_id=to, device_id_type=MESH
-        )
-        copy.start()
-        sent.append(copy)
-        return copy
-
-    copies = []
-    for step in (2, 1, 3):
-        to = lax.rem(y + step, SIDE)
-        copies.append(push(
-            part_ref.at[pl.ds(to * rows, rows)], col_buf.at[step - 1], col_s.at[step - 1], col_r.at[step - 1],
-            (lax.axis_index("row"), to),
-        ))
-    total = part_ref[pl.ds(y * rows, rows), :]
-    for copy in copies:
-        copy.wait_recv()
-    total = total + (col_buf[0] + col_buf[1] + col_buf[2])
-    slab_ref[...] = total
-    local_ref[...] = lax.dot_general(
-        total, total, (((0,), (0,)), ((), ())), precision=HIGHEST, preferred_element_type=jnp.float32
-    )
-
-    copies = []
-    for step in range(1, 8):
-        to, number = octet(step)
-        copies.append(push(
-            local_ref.at[pl.ds(number * strip, strip)], pair_buf.at[step - 1], pair_s.at[step - 1],
-            pair_r.at[step - 1], to,
-        ))
-    part = local_ref[pl.ds(me8 * strip, strip), :]
-    for step, copy in enumerate(copies):
-        copy.wait_recv()
-        part = part + pair_buf[step]
-
-    for here, buf, send, recv, peer in ((x, x_buf, x_s, x_r, along_x), (z, z_buf, z_s, z_r, along_z)):
-        buf[pl.ds(here, 1)] = part[None]
-        copies = []
-        for step in range(1, SIDE):
-            copies.append(push(buf.at[here], buf.at[here], send.at[step - 1], recv.at[step - 1], peer(step)))
-        for copy in copies:
-            copy.wait_recv()
-        part = (buf[0] + buf[1]) + (buf[2] + buf[3])
-
-    mine = pl.ds(me8 * strip, strip)
-    gram_ref[mine, :] = part
-    for step in range(1, 8):
-        to, number = octet(step)
-        push(gram_ref.at[mine], gram_ref.at[mine], last_s.at[step - 1], last_r.at[step - 1], to)
-    for copy in sent[-7:]:
-        copy.wait_recv()
-    for copy in sent:
-        copy.wait_send()
-
-
-def reduce(partial):
-    rows = partial.shape[0] // SIDE
-    dma = pltpu.SemaphoreType.DMA
-    strip = RANK // 8
-    f32 = jnp.float32
-    return pl.pallas_call(
-        reduce_kernel,
-        out_shape=(jax.ShapeDtypeStruct((rows, RANK), f32), jax.ShapeDtypeStruct((RANK, RANK), f32)),
-        in_specs=[pl.BlockSpec(memory_space=pltpu.VMEM)],
-        out_specs=(pl.BlockSpec(memory_space=pltpu.VMEM),) * 2,
-        scratch_shapes=[
-            pltpu.VMEM((RANK, RANK), f32),
-            pltpu.VMEM((3, rows, RANK), f32),
-            pltpu.VMEM((7, strip, RANK), f32),
-            pltpu.VMEM((SIDE, strip, RANK), f32),
-            pltpu.VMEM((SIDE, strip, RANK), f32),
-            dma((3,)), dma((3,)), dma((7,)), dma((7,)), dma((3,)), dma((3,)), dma((3,)), dma((3,)), dma((7,)), dma((7,)),
-        ],
-        compiler_params=pltpu.CompilerParams(collective_id=1, has_side_effects=True),
-    )(partial)
 
 
 def factor_kernel(gram_ref, slab_ref, basis_ref, factor_ref):
@@ -366,8 +346,7 @@
 
 
 def shards(blocks, block_row, block_col, sketch):
-    partial = sample(blocks, block_row, block_col, sketch)
-    slab, gram = reduce(partial.reshape(BR_DEV * BLK, RANK))
+    slab, gram = sample(blocks, block_row, block_col, sketch)
     return factorise(gram, slab)
 
 

time: 134 us -> 129 us (0.963)
  Pallas kernels: 134 us -> 128 us
    pallas_call x2 -> x1, Pallas kernels: 128 us -> 123 us  [sample(): pl.pallas_call(sampled_kernel, out_shape=(jax.ShapeDtypeStruct((BR_DEV *...]
where the time goes in v3:
time: 129 us
  Pallas kernels  128 us (99%)
    pallas_call x1, Pallas kernels, sample(): pl.pallas_call(sampled_kernel, out_shape=(jax.ShapeDtypeStruct((BR_DEV *...  123 us
    pallas_call x1, Pallas kernels, factorise(): pl.pallas_call(factor_kernel, out_shape=(jax.ShapeDtypeStruct(slab.shape,...  5.78 us

profile of v3, /device:TPU:1, one launch (start us, length us, event | category | flops | bytes accessed | tf_op | source)
XLA Modules:
  0.0 129.1 jit_solution(11980076487067319224)
XLA Ops:
  0.6 122.7 %shard_map.59 = (f32[256,128]{1,0:T(8,128)}, f32[128,128]{1,0:T(8,128)}) custom-call(s32[512]{0:T(512)} %row_ref.1, s32[512]{0:T(512)} %col_ref.1, bf16[32,16,128,128]{3,2,1,0:T(8,128)(2,1)} %bitcast.2, bf16[32,128,128]{2,1,0:T(8,128)(2,1)} %bitcast.3), custom_call_target="tpu_custom_call" | custom-call | tf_op jit(solution)/shard_map/pallas_call | solution.py:252
  123.3 5.8 %shard_map.60 = (f32[256,128]{1,0:T(8,128)}, f32[128,128]{1,0:T(8,128)}) custom-call(f32[128,128]{1,0:T(8,128)} %get-tuple-element.4.gram_ref, f32[256,128]{1,0:T(8,128)} %get-tuple-element.5.slab_ref), custom_call_target="tpu_custom_call" | custom-call | tf_op jit(solution)/shard_map/pallas_call | solution.py:339

commit v4 on v3

--- a/solution.py
+++ b/solution.py
@@ -12,6 +12,7 @@
 RANK = 128
 BR_DEV = 8
 CAP = 16
+SHIFT = 5
 SIDE = 4
 HIGHEST = lax.Precision.HIGHEST
 
@@ -45,7 +46,7 @@
 )
 
 
-def sampled_kernel(row_ref, col_ref, blocks_ref, mine_ref, slab_ref, gram_ref, *scratch):
+def sampled_kernel(slot_ref, blocks_ref, mine_ref, slab_ref, gram_ref, *scratch):
     held = {(c // SIDE, c % SIDE): scratch[c] for c in range(SIDE * SIDE)}
     stored, chain, total_ref, local_ref, col_buf, octet_buf, plane_buf, *scratch = scratch[SIDE * SIDE :]
     block_sem, own_sem, send_sem, recv_sem, pair_send, pair_recv, *scratch = scratch
@@ -125,8 +126,8 @@
             group = row_of(lax.rem(z - dz + SIDE, SIDE), lax.rem(x - dx + SIDE, SIDE), lax.rem(core + plane, 2))
             last = [CAP] * BR_DEV
             for k in range(CAP):
-                row = row_ref[group * CAP + k]
-                col = jnp.maximum(col_ref[group * CAP + k], 0)
+                code = slot_ref[group * CAP + k]
+                row, col = code >> SHIFT, code & (2**SHIFT - 1)
                 before = CAP
                 for b in range(BR_DEV):
                     same = row == b
@@ -257,7 +258,6 @@
         ),
         in_specs=[
             pl.BlockSpec(memory_space=pltpu.SMEM),
-            pl.BlockSpec(memory_space=pltpu.SMEM),
             pl.BlockSpec(memory_space=pl.ANY),
             pl.BlockSpec(memory_space=pl.ANY),
         ],
@@ -287,9 +287,9 @@
             dma((7,)),
         ],
         compiler_params=pltpu.CompilerParams(
-            collective_id=0, has_side_effects=True, vmem_limit_bytes=58 * 2**20
+            collective_id=0, has_side_effects=True, vmem_limit_bytes=53 * 2**20
         ),
-    )(block_row, block_col, blocks.reshape(groups, CAP, BLK, BLK), sketch.reshape(count, BLK, RANK))
+    )((block_row << SHIFT) + block_col, blocks.reshape(groups, CAP, BLK, BLK), sketch.reshape(count, BLK, RANK))
 
 
 def factor_kernel(gram_ref, slab_ref, basis_ref, factor_ref):
@@ -342,6 +342,9 @@
             jax.ShapeDtypeStruct(slab.shape, jnp.float32),
             jax.ShapeDtypeStruct(gram.shape, jnp.float32),
         ),
+        in_specs=[pl.BlockSpec(memory_space=pltpu.VMEM)] * 2,
+        out_specs=(pl.BlockSpec(memory_space=pltpu.VMEM),) * 2,
+        compiler_params=pltpu.CompilerParams(vmem_limit_bytes=8 * 2**20),
     )(gram, slab)
 
 

time: 129 us -> 128 us (level)
  no operation moved by 1% of the time
where the time goes in v4:
time: 128 us
  Pallas kernels  127 us (99%)
    pallas_call x1, Pallas kernels, sample(): pl.pallas_call(sampled_kernel, out_shape=(jax.ShapeDtypeStruct((BR_DEV *...  122 us
    pallas_call x1, Pallas kernels, factorise(): pl.pallas_call(factor_kernel, out_shape=(jax.ShapeDtypeStruct(slab.shape,...  4.83 us

profile of v4, /device:TPU:1, one launch (start us, length us, event | category | flops | bytes accessed | tf_op | source)
XLA Modules:
  0.0 128.2 jit_solution(18262393904716984047)
XLA Ops:
  0.6 0.7 shift-left_add_fusion.slot_ref
  1.3 122.0 %shard_map.59 = (f32[256,128]{1,0:T(8,128)S(1)}, f32[128,128]{1,0:T(8,128)S(1)}) custom-call(s32[512]{0:T(512)S(1)} %shift-left_add_fusion.slot_ref, bf16[32,16,128,128]{3,2,1,0:T(8,128)(2,1)} %bitcast.2, bf16[32,128,128]{2,1,0:T(8,128)(2,1)} %bitcast.3), custom_call_target="tpu_custom_call" | custom-call | tf_op jit(solution)/shard_map/pallas_call | solution.py:253
  123.4 4.8 %shard_map.60 = (f32[256,128]{1,0:T(8,128)}, f32[128,128]{1,0:T(8,128)}) custom-call(f32[128,128]{1,0:T(8,128)S(1)} %get-tuple-element.4.gram_ref, f32[256,128]{1,0:T(8,128)S(1)} %get-tuple-element.5.slab_ref), custom_call_target="tpu_custom_call" | custom-call | tf_op jit(solution)/shard_map/pallas_call | solution.py:339

commit v5 on v4

--- a/solution.py
+++ b/solution.py
@@ -40,9 +40,9 @@
     ((3, 1),),
     ((3, 3),),
     (),
-    ((0, 2), (2, 0)),
-    ((1, 2), (2, 1)),
+    ((0, 2), (2, 0), (1, 2), (2, 1)),
     ((3, 2), (2, 3)),
+    (),
 )
 
 

time: 128 us -> 128 us (level)
  no operation moved by 1% of the time
where the time goes in v5:
time: 128 us
  Pallas kernels  126 us (98%)
    pallas_call x1, Pallas kernels, sample(): pl.pallas_call(sampled_kernel, out_shape=(jax.ShapeDtypeStruct((BR_DEV *...  122 us
    pallas_call x1, Pallas kernels, factorise(): pl.pallas_call(factor_kernel, out_shape=(jax.ShapeDtypeStruct(slab.shape,...  4.83 us

profile of v5, /device:TPU:1, one launch (start us, length us, event | category | flops | bytes accessed | tf_op | source)
XLA Modules:
  0.0 127.8 jit_solution(9430838107411639842)
XLA Ops:
  0.6 0.7 shift-left_add_fusion.slot_ref
  1.3 121.6 %shard_map.59 = (f32[256,128]{1,0:T(8,128)S(1)}, f32[128,128]{1,0:T(8,128)S(1)}) custom-call(s32[512]{0:T(512)S(1)} %shift-left_add_fusion.slot_ref, bf16[32,16,128,128]{3,2,1,0:T(8,128)(2,1)} %bitcast.2, bf16[32,128,128]{2,1,0:T(8,128)(2,1)} %bitcast.3), custom_call_target="tpu_custom_call" | custom-call | tf_op jit(solution)/shard_map/pallas_call | solution.py:253
  122.9 4.8 %shard_map.60 = (f32[256,128]{1,0:T(8,128)}, f32[128,128]{1,0:T(8,128)}) custom-call(f32[128,128]{1,0:T(8,128)S(1)} %get-tuple-element.4.gram_ref, f32[256,128]{1,0:T(8,128)S(1)} %get-tuple-element.5.slab_ref), custom_call_target="tpu_custom_call" | custom-call | tf_op jit(solution)/shard_map/pallas_call | solution.py:339
